TPU v7x, 512 devices: a whole 4x4x16 slice. The times are simulated.
512 devices in a mesh: row: 16 (over x, z_hi, core), col: 32 (over z_lo, y).
Axes of the slice: x: 4, y: 4, z: 16 (z_hi: 2, z_lo: 8; z = z_hi * 8 + z_lo), core: 2. Of those that a mesh axis runs over, the one named last changes fastest.
Arguments:
- output_gradient: bfloat16 [512, 16384], P('col', 'row'), may hold values from -6 to 6
- codes: bfloat16 [53248, 16384], P('col', 'row'), may hold values from -4 to 4
- feature_scale: float32 [16384], P('row'), may hold values from 0.002 to 0.02
- adapter_down_map: bfloat16 [16, 53248], P(None, 'col'), may hold values from -1.5 to 1.5
- adapter_up_map: bfloat16 [16, 16384], P(None, 'row'), may hold values from -0.046875 to 0.046875
- stored_activation: bfloat16 [512, 53248], P('row', 'col'), may hold values from -1 to 1
Outputs:
- activation_derivative: bfloat16 [512, 53248], P('row', 'col')
- compress_matrix_derivative: float32 [16, 53248], P(None, ('col', 'row'))
All inputs are finite; a program needn't handle non-finite values.
Results may differ from a plain program's by a relative error of at most 0.0049.
Values may be sent and summed in bfloat16 or wider, within the bound.
A program may use at most 64 MiB of HBM per device.

v0:
```python
import jax
import jax.numpy as jnp
from jax import lax
from jax.sharding import PartitionSpec as P

correction_multiplier = 0.5


def on_device(
    output_gradient, codes, feature_scale, adapter_down_map, adapter_up_map, stored_activation
):
    resident_compressed = lax.dot_general(
        output_gradient,
        adapter_up_map,
        (((1,), (1,)), ((), ())),
        preferred_element_type=jnp.float32,
    )
    bottleneck_derivative = lax.psum(resident_compressed, "row")
    bottleneck_derivative_narrowed = lax.all_gather(
        bottleneck_derivative.astype(jnp.bfloat16), "col", axis=0, tiled=True
    )
    row_count = stored_activation.shape[0]
    resident_slice_height = lax.dynamic_slice_in_dim(
        bottleneck_derivative_narrowed, lax.axis_index("row") * row_count, row_count, 0
    )
    whole = lax.all_gather(output_gradient, "col", axis=0, tiled=True)
    scaled = (whole.astype(jnp.float32) * feature_scale[None, :]).astype(jnp.bfloat16)
    main_branch = lax.psum_scatter(
        lax.dot_general(
            scaled, codes, (((1,), (1,)), ((), ())), preferred_element_type=jnp.float32
        ),
        "row",
        scatter_dimension=0,
        tiled=True,
    )
    adapter_term = jnp.dot(
        resident_slice_height, adapter_down_map, preferred_element_type=jnp.float32
    )
    activation_derivative = (main_branch + correction_multiplier * adapter_term).astype(
        jnp.bfloat16
    )
    partial_adapter_gradient = correction_multiplier * lax.dot_general(
        resident_slice_height,
        stored_activation,
        (((0,), (0,)), ((), ())),
        preferred_element_type=jnp.float32,
    )
    compress_matrix_derivative = lax.psum_scatter(
        partial_adapter_gradient, "row", scatter_dimension=1, tiled=True
    )
    return (activation_derivative, compress_matrix_derivative)


def solution(mesh):
    return jax.shard_map(
        on_device,
        mesh=mesh,
        in_specs=(
            P("col", "row"),
            P("col", "row"),
            P("row"),
            P(None, "col"),
            P(None, "row"),
            P("row", "col"),
        ),
        out_specs=(P("row", "col"), P(None, ("col", "row"))),
        check_vma=False,
    )
```

profile of v0, /device:TPU:24, one launch (start us, length us, event | category | flops | bytes accessed | tf_op | source)
XLA Modules:
  0.0 596.6 jit_solution(6127790067411689030)
XLA Ops:
  8.0 0.0 copy-start
  8.0 0.0 all-gather.2.cloned.1.call-start
  8.1 0.7 all-gather.2.cloned.1.call-update
  8.7 0.0 all-reduce.3.cloned.1.call-start
  8.8 1.1 fusion.8
  9.9 78.0 %psum.7 = bf16[16,16]{1,0:T(8,128)(2,1)S(1)} all-reduce(f32[16,16]{1,0:T(8,128)S(1)} %fusion.8), channel_id=1, replica_groups=mesh['row'=16,'col'=32] {'row'}, use_global_device_ids=true, to_apply=%region_1.0 | all-reduce | flops 256 | bytes 1536 | tf_op jit(solution)/shard_map/psum | solution.py:18
  88.0 102.7 %all_gather.7 = bf16[512,16]{1,0:T(8,128)(2,1)S(1)} all-gather(bf16[16,16]{1,0:T(8,128)(2,1)S(1)} %psum.7), channel_id=1, replica_groups=mesh['row'=16,'col'=32] {'col'}, dimensions={0}, use_global_device_ids=true | all-gather | bytes 16896 | tf_op jit(solution)/shard_map/all_gather | solution.py:19
  190.6 1.7 convolution_multiply_fusion.1
  192.4 0.0 all-reduce.3.cloned.1.call-update
  192.4 0.0 reduce-scatter.3.cloned.1.call-start
  192.4 35.5 %all-gather.2.cloned.1.call-done = bf16[512,1024]{1,0:T(8,128)(2,1)} async-done(((bf16[16,1024]{1,0:T(8,128)(2,1)}), bf16[512,1024]{1,0:T(8,128)(2,1)}) %all-gather.2.cloned.1.call-update) | async-done | bytes 1048592 | tf_op jit(solution)/shard_map/all_gather | solution.py:26
  227.9 0.0 copy-done
  227.9 5.1 fusion.2
  233.0 0.0 reduce-scatter.3.cloned.1.call-update
  233.0 1.3 dynamic-slice
  234.9 206.9 %all-reduce.3.cloned.1.call-done = f32[16,1664]{1,0:T(8,128)} async-done(((f32[16,1664]{1,0:T(8,128)}), f32[16,1664]{1,0:T(8,128)}) %all-reduce.3.cloned.1.call-update) | async-done | bytes 106512
  441.8 1.4 constant_dynamic-slice_fusion
  443.2 144.2 %reduce-scatter.3.cloned.1.call-done = f32[32,1664]{1,0:T(8,128)} async-done(((f32[512,1664]{1,0:T(8,128)}), f32[32,1664]{1,0:T(8,128)}) %reduce-scatter.3.cloned.1.call-update) | async-done | bytes 213008 | tf_op jit(solution)/shard_map/reduce_scatter | solution.py:28
  587.4 1.8 fusion.1
Async XLA Ops:
  8.0 219.9 %copy-start = (bf16[1664,1024]{1,0:T(8,128)(2,1)S(1)}, bf16[1664,1024]{1,0:T(8,128)(2,1)}, u32[]{:S(2)}) copy-start(bf16[1664,1024]{1,0:T(8,128)(2,1)} %param.7) | copy-start | bytes 10223620
  8.0 219.9 %all-gather.2.cloned.1.call-start = ((), (), s32[]{:S(2)}) async-start(), calls=%async_computation.1 | async-start | bytes 1081344 | tf_op jit(solution)/shard_map/all_gather | solution.py:26
  8.7 433.1 %all-reduce.3.cloned.1.call-start = ((), (), s32[]{:S(2)}) async-start(), calls=%async_computation.3 | async-start | bytes 212992
  192.4 395.0 %reduce-scatter.3.cloned.1.call-start = ((), (), s32[]{:S(2)}) async-start(), calls=%async_computation.2 | async-start | bytes 3620864 | tf_op jit(solution)/shard_map/reduce_scatter | solution.py:28
Sparse Core Ops, SparseCore 0:
  11.1 216.7 all-gather.1
Sparse Core Ops, SparseCore 1:
  192.5 249.3 all-reduce.2
  447.4 140.0 reduce-scatter.2
where the time goes:
time: 597 us
  waiting for transfers between devices  387 us (65%)
  blocking collectives  181 us (30%)
  between operations  16.2 us (3%)
  matrix products  9.68 us (2%)
    unnamed x4, waiting for transfers between devices  208 us
    reduce_scatter x1, waiting for transfers between devices, on_device(): lax.psum_scatter(lax.dot_general(scaled, codes, (((1,), (1,)), ((), ())),...  144 us
    all_gather x1, blocking collectives, on_device(): lax.all_gather(bottleneck_derivative.astype(jnp.bfloat16), 'col', axis=0,...  103 us
    psum x1, blocking collectives, on_device(): bottleneck_derivative = lax.psum(resident_compressed, 'row')  78 us
    all_gather x1, waiting for transfers between devices, on_device(): whole = lax.all_gather(output_gradient, 'col', axis=0, tiled=True)  35.5 us
  transfers between devices with their start and end apart: 3, of which 3 were waited for; matrix products, arithmetic and copies ran while one was open for 2% of the time, Pallas kernels for 0%

commit v1 on v0

v1 whole, which is shorter than its diff:
```python
import jax
import jax.numpy as jnp
from jax import lax
from jax.experimental import pallas as pl
from jax.experimental.pallas import tpu as pltpu
from jax.sharding import PartitionSpec as P

MESH = pl.DeviceIdType.MESH
F32, BF16 = jnp.float32, jnp.bfloat16
GROUPS = ((0, 512), (512, 512), (1024, 640))
NG = len(GROUPS)
SLICE = 104


def flip(v, b):
    return v + b - 2 * b * lax.rem(lax.div(v, b), 2)


def dot_nt(a, b):
    return lax.dot_general(a, b, (((1,), (1,)), ((), ())), preferred_element_type=F32)


def kernel(
    grad, codes, scale, down, up, act, out, comp,
    gbuf, codes_v, scale_v, down_v, up_v, act_v, lhs, acc, psend, precv, xsend, xrecv, zsend, zrecv,
    low, lprecv, lxrecv, lzrecv, cblk, cprecv, cxrecv, czrecv,
    lsem, gzs, gzr, gys, gyr, pss, psr, xss, xsr, zss, zsr,
    lps, lpr, lxs, lxr, lzs, lzr, cps, cpr, cxs, cxr, czs, czr,
):
    row, col = lax.axis_index("row"), lax.axis_index("col")
    core, zh, x = lax.rem(row, 2), lax.rem(lax.div(row, 2), 2), lax.div(row, 4)
    y, zl = lax.rem(col, 4), lax.div(col, 4)

    def at_row(x_, zh_, core_):
        return {"row": x_ * 4 + zh_ * 2 + core_, "col": col}

    def at_col(zl_, y_):
        return {"row": row, "col": zl_ * 4 + y_}

    mate = at_row(x, zh, 1 - core)
    far = at_row(x, 1 - zh, core)
    xs = [lax.rem(x + j, 4) for j in (1, 2, 3)]
    x_peer = [at_row(v, zh, core) for v in xs]
    y_peer = [at_col(zl, lax.rem(y + j, 4)) for j in (1, 2, 3)]
    z_peer = {b: at_col(flip(zl, b), y) for b in (1, 2, 4)}

    def rc(src, dst, ss, rs, dev):
        return pltpu.make_async_remote_copy(
            src_ref=src, dst_ref=dst, send_sem=ss, recv_sem=rs, device_id=dev, device_id_type=MESH
        )

    local = [
        pltpu.make_async_copy(s, d, lsem.at[i])
        for i, (s, d) in enumerate(
            ((grad, gbuf.at[col]), (scale, scale_v), (up, up_v), (codes, codes_v), (down, down_v), (act, act_v))
        )
    ]
    for c in local:
        c.start()

    barrier = pltpu.get_barrier_semaphore()
    peers = [mate, far, *x_peer, *y_peer, *z_peer.values()]
    for p in peers:
        pl.semaphore_signal(barrier, inc=1, device_id=p, device_id_type=MESH)
    pl.semaphore_wait(barrier, len(peers))
    local[0].wait()

    sends = []

    def zmap(m):
        v = zl
        for b in (1, 2, 4):
            if m & b:
                v = flip(v, b)
        return v

    def pass_on(m, bits):
        k = zmap(m)
        c = k * 4 + y
        for b in bits:
            d = rc(gbuf.at[c], gbuf.at[c], gzs.at[m ^ b], gzr.at[m ^ b], z_peer[b])
            d.start()
            sends.append(d)
        for j in range(3):
            d = rc(gbuf.at[c], gbuf.at[c], gys.at[k, j], gyr.at[k, j], y_peer[j])
            d.start()
            sends.append(d)

    def z_wait(m):
        c = zmap(m) * 4 + y
        rc(gbuf.at[c], gbuf.at[c], gzs.at[m], gzr.at[m], z_peer[1]).wait_recv()

    pass_on(0, (4, 2, 1))
    for m, bits in ((4, (2, 1)), (2, (1,)), (1, ()), (6, (1,)), (5, ()), (3, ()), (7, ())):
        z_wait(m)
        pass_on(m, bits)

    for c in local[1:3]:
        c.wait()

    def y_wait(par):
        for v in range(4):
            k = 2 * v + par
            for j in range(3):
                c = k * 4 + lax.rem(y + 3 - j, 4)
                rc(gbuf.at[c], gbuf.at[c], gys.at[k, j], gyr.at[k, j], y_peer[j]).wait_recv()

    def prepare(q, par):
        for i, c_ in enumerate((1 - core, core)):
            for v in range(4):
                g = gbuf[pl.ds((2 * v + par) * 4 + 2 * c_, 2)].reshape(32, 1024)
                low[q, i, v, :, 0:32] = dot_nt(up_v[...], g)
                lhs[i, v * 32 : v * 32 + 32, :] = (g.astype(F32) * scale_v[...]).astype(BF16)

    def pair_copies(q):
        return [
            rc(psend.at[q, :, :, pl.ds(n, w)], precv.at[q, :, :, pl.ds(n, w)], pss.at[q, s], psr.at[q, s], mate)
            for s, (n, w) in enumerate(GROUPS)
        ]

    def low_pair(q):
        return rc(low.at[q, 0], lprecv.at[q], lps.at[q], lpr.at[q], mate)

    def x_copies(q, s):
        n, w = GROUPS[s]
        return [
            rc(
                xsend.at[q, xs[j], :, pl.ds(n, w)], xrecv.at[q, j, :, pl.ds(n, w)],
                xss.at[q, s, j], xsr.at[q, s, j], x_peer[j],
            )
            for j in range(3)
        ]

    def low_x(q):
        return [
            rc(low.at[q, 1, xs[j]], lxrecv.at[q, j], lxs.at[q, j], lxr.at[q, j], x_peer[j]) for j in range(3)
        ]

    def multiply(q):
        low_pair(q).start()
        copies = pair_copies(q)
        for s, (n, w) in enumerate(GROUPS):
            r = dot_nt(lhs[0], codes_v[n : n + w, :])
            psend[q, :, :, n : n + w] = r.astype(BF16).reshape(4, 32, w)
            copies[s].start()
        for s, (n, w) in enumerate(GROUPS):
            acc[q, :, :, n : n + w] = dot_nt(lhs[1], codes_v[n : n + w, :]).reshape(4, 32, w)

    def to_x(q):
        low_pair(q).wait_recv()
        low[q, 1] = low[q, 1] + lprecv[q]
        for d in low_x(q):
            d.start()
        copies = pair_copies(q)
        for s, (n, w) in enumerate(GROUPS):
            copies[s].wait_recv()
            v = acc[q, :, :, n : n + w] + precv[q, :, :, n : n + w].astype(F32)
            acc[q, :, :, n : n + w] = v
            xsend[q, :, :, n : n + w] = v.astype(BF16)
            for d in x_copies(q, s):
                d.start()

    def x_sum(q, s):
        n, w = GROUPS[s]
        for d in x_copies(q, s):
            d.wait_recv()
        v = acc[q, pl.ds(x, 1), :, n : n + w].reshape(32, w)
        for j in range(3):
            v = v + xrecv[q, j, :, n : n + w].astype(F32)
        return v

    def low_sum(q):
        for d in low_x(q):
            d.wait_recv()
        v = low[q, 1, pl.ds(x, 1)].reshape(16, 128)
        for j in range(3):
            v = v + lxrecv[q, j]
        return v

    low_far = rc(low.at[0, 0, 0], lzrecv, lzs, lzr, far)
    z_copies = [
        rc(zsend.at[:, pl.ds(n, w)], zrecv.at[:, pl.ds(n, w)], zss.at[s], zsr.at[s], far)
        for s, (n, w) in enumerate(GROUPS)
    ]

    low[...] = jnp.zeros_like(low)
    y_wait(1 - zh)
    prepare(0, 1 - zh)
    local[3].wait()
    multiply(0)
    to_x(0)
    y_wait(zh)
    prepare(1, zh)
    multiply(1)
    low_pair(0).wait_send()
    low[0, 0, 0] = low_sum(0)
    low_far.start()
    for s, (n, w) in enumerate(GROUPS):
        zsend[:, n : n + w] = x_sum(0, s).astype(BF16)
        z_copies[s].start()
    to_x(1)

    v = low_sum(1)
    low_far.wait_recv()
    rounded = (v + lzrecv[...]).astype(BF16)[:, 0:32]
    for c in local[4:]:
        c.wait()
    part = 0.5 * jnp.dot(rounded, act_v[...], preferred_element_type=F32)
    for r in range(16):
        start = r * SLICE
        base, off = start // 128 * 128, start % 128
        if off + SLICE <= 128:
            b = part[:, base : base + 128]
            b = pltpu.roll(b, (128 - off) % 128, 1) if off else b
        else:
            b = pltpu.roll(part[:, base : base + 256], 256 - off, 1)[:, 0:128]
        cblk[r % 2, r // 4, (r // 2) % 2] = b
    c_pair = rc(cblk.at[1 - core], cprecv, cps, cpr, mate)
    c_pair.start()

    for s, (n, w) in enumerate(GROUPS):
        term = lax.dot_general(
            rounded, down_v[:, n : n + w], (((0,), (0,)), ((), ())), preferred_element_type=F32
        )
        acc[0, 0, :, n : n + w] = x_sum(1, s) + 0.5 * term
        if s == 0:
            c_pair.wait_recv()
            cblk[pl.ds(core, 1)] = cblk[pl.ds(core, 1)] + cprecv[...][None]
            c_x = [rc(cblk.at[core, xs[j]], cxrecv.at[j], cxs.at[j], cxr.at[j], x_peer[j]) for j in range(3)]
            for d in c_x:
                d.start()

    for d in c_x:
        d.wait_recv()
    v = cblk[pl.ds(core, 1), pl.ds(x, 1)].reshape(2, 16, 128)
    for j in range(3):
        v = v + cxrecv[j]
    c_pair.wait_send()
    cblk[pl.ds(1 - core, 1), 0] = v[None]
    c_far = rc(cblk.at[1 - core, 0, 1 - zh], czrecv, czs, czr, far)
    c_far.start()

    for s, (n, w) in enumerate(GROUPS):
        z_copies[s].wait_recv()
        out[:, n : n + w] = (acc[0, 0, :, n : n + w] + zrecv[:, n : n + w].astype(F32)).astype(BF16)
    c_far.wait_recv()
    keep = cblk[pl.ds(1 - core, 1), 0, pl.ds(zh, 1)].reshape(16, 128)
    comp[...] = (keep + czrecv[...])[:, 0:SLICE]

    for d in sends:
        d.wait_send()
    low_pair(1).wait_send()
    for q in range(2):
        for d in pair_copies(q) + low_x(q):
            d.wait_send()
        for s in range(NG):
            for d in x_copies(q, s):
                d.wait_send()
    for d in [low_far, c_far, *c_x, *z_copies]:
        d.wait_send()


def on_device(grad, codes, scale, down, up, act):
    hidden, width = codes.shape
    any_ = pl.BlockSpec(memory_space=pl.ANY)
    vmem = pl.BlockSpec(memory_space=pltpu.VMEM)
    dma = pltpu.SemaphoreType.DMA
    out, comp = pl.pallas_call(
        kernel,
        out_shape=(
            jax.ShapeDtypeStruct((32, hidden), BF16),
            jax.ShapeDtypeStruct((16, SLICE), F32),
        ),
        in_specs=[any_] * 6,
        out_specs=(vmem, vmem),
        scratch_shapes=[
            pltpu.VMEM((32, 16, width), BF16),
            pltpu.VMEM((hidden, width), BF16),
            pltpu.VMEM((1, width), F32),
            pltpu.VMEM((16, hidden), BF16),
            pltpu.VMEM((16, width), BF16),
            pltpu.VMEM((32, hidden), BF16),
            pltpu.VMEM((2, 128, width), BF16),
            pltpu.VMEM((2, 4, 32, hidden), F32),
            pltpu.VMEM((2, 4, 32, hidden), BF16),
            pltpu.VMEM((2, 4, 32, hidden), BF16),
            pltpu.VMEM((2, 4, 32, hidden), BF16),
            pltpu.VMEM((2, 3, 32, hidden), BF16),
            pltpu.VMEM((32, hidden), BF16),
            pltpu.VMEM((32, hidden), BF16),
            pltpu.VMEM((2, 2, 4, 16, 128), F32),
            pltpu.VMEM((2, 4, 16, 128), F32),
            pltpu.VMEM((2, 3, 16, 128), F32),
            pltpu.VMEM((16, 128), F32),
            pltpu.VMEM((2, 4, 2, 16, 128), F32),
            pltpu.VMEM((4, 2, 16, 128), F32),
            pltpu.VMEM((3, 2, 16, 128), F32),
            pltpu.VMEM((16, 128), F32),
            dma((6,)),
            dma((8,)), dma((8,)), dma((8, 3)), dma((8, 3)),
            dma((2, NG)), dma((2, NG)), dma((2, NG, 3)), dma((2, NG, 3)), dma((NG,)), dma((NG,)),
            dma((2,)), dma((2,)), dma((2, 3)), dma((2, 3)), dma, dma,
            dma, dma, dma((3,)), dma((3,)), dma, dma,
        ],
        compiler_params=pltpu.CompilerParams(
            collective_id=0, has_side_effects=True, vmem_limit_bytes=60 * 2**20
        ),
        cost_estimate=pl.CostEstimate(flops=2 * 512 * hidden * width, bytes_accessed=4 * 2**20, transcendentals=0),
    )(grad, codes, scale.reshape(1, width), down, up, act)
    return out, comp


def solution(mesh):
    return jax.shard_map(
        on_device,
        mesh=mesh,
        in_specs=(
            P("col", "row"),
            P("col", "row"),
            P("row"),
            P(None, "col"),
            P(None, "row"),
            P("row", "col"),
        ),
        out_specs=(P("row", "col"), P(None, ("col", "row"))),
        check_vma=False,
    )
```

time: 597 us -> 64.2 us (0.11)
  the two profiles are of different devices: /device:TPU:24 before, /device:TPU:1 now
where the time goes in v1:
time: 64.2 us; the launch traced here: 64.1 us
  Pallas kernels  60.6 us (94%)
  local copies, waits for them, and re-layouts  2.84 us (4%)
    pallas_call x1, Pallas kernels, on_device(): pl.pallas_call(kernel, out_shape=(jax.ShapeDtypeStruct((32, hidden), BF16...  60.6 us
    unnamed x2, local copies, waits for them, and re-layouts  2.84 us

profile of v1, /device:TPU:1, one launch (start us, length us, event | category | flops | bytes accessed | tf_op | source)
XLA Modules:
  0.0 64.1 jit_solution(16599293141789374136)
XLA Ops:
  0.6 60.6 %shard_map.77 = (bf16[32,1664]{1,0:T(8,128)(2,1)}, f32[16,104]{1,0:T(8,128)}) custom-call(bf16[16,1024]{1,0:T(8,128)(2,1)} %grad.1, bf16[1664,1024]{1,0:T(8,128)(2,1)} %codes.1, f32[1,1024]{1,0:T(1,128)} %bitcast.1, bf16[16,1664]{1,0:T(8,128)(2,1)} %down.1, bf16[16,1024]{1,0:T(8,128)(2,1)} %up.1, bf16[32,1664]{1,0:T(8,128)(2,1)} %act.1), custom_call_target="tpu_custom_call" | custom-call | flops 1744830464 | bytes 4194304 | tf_op jit(solution)/shard_map/pallas_call | solution.py:268
  61.2 1.5 %copy.10 = bf16[32,1664]{1,0:T(8,128)(2,1)} copy(bf16[32,1664]{1,0:T(8,128)(2,1)} %get-tuple-element.4) | data formatting | bytes 212992
  62.8 1.3 %copy.11 = f32[16,104]{1,0:T(8,128)} copy(f32[16,104]{1,0:T(8,128)} %get-tuple-element.5) | data formatting | bytes 13312

commit v2 on v1

v2 whole, which is shorter than its diff:
```python
import jax
import jax.numpy as jnp
from jax import lax
from jax.experimental import pallas as pl
from jax.experimental.pallas import tpu as pltpu
from jax.sharding import PartitionSpec as P

MESH = pl.DeviceIdType.MESH
F32, BF16 = jnp.float32, jnp.bfloat16
GROUPS = ((0, 768), (768, 896))
NG = len(GROUPS)
SLICE = 104
RANK = 16


def flip(v, b):
    return v + b - 2 * b * lax.rem(lax.div(v, b), 2)


def dot_nt(a, b):
    return lax.dot_general(a, b, (((1,), (1,)), ((), ())), preferred_element_type=F32)


def dot_tn(a, b):
    return lax.dot_general(a, b, (((0,), (0,)), ((), ())), preferred_element_type=F32)


def kernel(
    grad, codes, scale, down, up, act, out, comp,
    gbuf, codes_v, codes_t, scale_v, down_v, up_v, act_v, lhs, acc, psend, precv, xsend, xrecv, zsend, zrecv, total,
    lsum, lmate, lx, lfar, low, cblk, cprecv, cxrecv, czsend, czrecv,
    far_in, lsem, gzs, gzr, gys, gyr, pss, psr, xss, xsr, zss, zsr,
    lps, lpr, lxs, lxr, lfs, lfr, lys, lyr, lzs, lzr, cps, cpr, cxs, cxr, czs, czr,
):
    row, col = lax.axis_index("row"), lax.axis_index("col")
    core, zh, x = lax.rem(row, 2), lax.rem(lax.div(row, 2), 2), lax.div(row, 4)
    y, zl = lax.rem(col, 4), lax.div(col, 4)

    def at_row(x_, zh_, core_):
        return {"row": x_ * 4 + zh_ * 2 + core_, "col": col}

    def at_col(zl_, y_):
        return {"row": row, "col": zl_ * 4 + y_}

    def zmap(m):
        v = zl
        for b in (1, 2, 4):
            if m & b:
                v = flip(v, b)
        return v

    mate = at_row(x, zh, 1 - core)
    far = at_row(x, 1 - zh, core)
    cross = {"row": x * 4 + (1 - zh) * 2 + core, "col": zmap(4) * 4 + y}
    xs = [lax.rem(x + j, 4) for j in (1, 2, 3)]
    x_peer = [at_row(v, zh, core) for v in xs]
    y_peer = [at_col(zl, lax.rem(y + j, 4)) for j in (1, 2, 3)]
    z_peer = {m: at_col(zmap(m), y) for m in (1, 2, 3, 4)}

    def rc(src, dst, ss, rs, dev):
        return pltpu.make_async_remote_copy(
            src_ref=src, dst_ref=dst, send_sem=ss, recv_sem=rs, device_id=dev, device_id_type=MESH
        )

    local = [
        pltpu.make_async_copy(s, d, lsem.at[i])
        for i, (s, d) in enumerate(
            ((grad, gbuf.at[col]), (scale, scale_v), (up, up_v), (codes, codes_v), (down, down_v), (act, act_v))
        )
    ]
    for c in local:
        c.start()

    barrier = pltpu.get_barrier_semaphore()
    peers = [z_peer[4], cross, z_peer[3], z_peer[2], z_peer[1], *x_peer, *y_peer, mate]
    for p in peers:
        pl.semaphore_signal(barrier, inc=1, device_id=p, device_id_type=MESH)
    local[0].wait()
    local[2].wait()
    lsum[...] = jnp.zeros_like(lsum)
    lsum[0, :, 0:RANK] = dot_nt(gbuf[pl.ds(col, 1)].reshape(16, -1), up_v[...])
    low_mate = rc(lsum.at[0], lmate, lps, lpr, mate)
    low_x = [rc(lsum.at[1], lx.at[j], lxs.at[j], lxr.at[j], x_peer[j]) for j in range(3)]
    low_far = rc(lsum.at[2], lfar, lfs, lfr, far)
    pl.semaphore_wait(barrier, len(peers))
    pl.semaphore_signal(far_in, inc=1, device_id=z_peer[4], device_id_type=MESH)

    sends = []

    def pass_on(m, bits):
        k = zmap(m)
        c = k * 4 + y
        for b in bits:
            d = rc(gbuf.at[c], gbuf.at[c], gzs.at[m ^ b], gzr.at[m ^ b], z_peer[b])
            d.start()
            sends.append(d)
        for j in range(3):
            d = rc(gbuf.at[c], gbuf.at[c], gys.at[k, j], gyr.at[k, j], y_peer[j])
            d.start()
            sends.append(d)

    def z_wait(m):
        c = zmap(m) * 4 + y
        rc(gbuf.at[c], gbuf.at[c], gzs.at[m], gzr.at[m], z_peer[1]).wait_recv()

    pass_on(0, (4, 3, 2, 1))
    low_mate.start()
    local[3].wait()
    for n in range(0, codes_v.shape[0], 128):
        codes_t[:, n : n + 128] = codes_v[n : n + 128, :].T
    z_wait(1)
    pass_on(1, ())
    low_mate.wait_recv()
    lsum[1] = lsum[0] + lmate[...]
    for d in low_x:
        d.start()
    for m in (2, 3):
        z_wait(m)
        pass_on(m, ())
    lsum[2] = lsum[1]
    for j in range(3):
        low_x[j].wait_recv()
        lsum[2] += lx[j]
    pl.semaphore_wait(far_in, 1)
    low_far.start()
    z_wait(4)
    pass_on(4, (3, 2, 1))
    for m in (5, 6, 7):
        z_wait(m)
        pass_on(m, ())

    at_source = zl == 2 * x + zh
    is_source = [at_source & (lax.div(y, 2) == core) & (lax.rem(y, 2) == b) for b in (0, 1)]
    low_y = [[rc(low.at[b], low.at[b], lys.at[b, j], lyr.at[b], y_peer[j]) for j in range(3)] for b in (0, 1)]
    low_z = [rc(low, low, lzs.at[m], lzr, at_col(zmap(m), y)) for m in range(1, 8)]

    def low_to_y():
        low_far.wait_recv()
        whole = (lsum[2] + lfar[...]).astype(BF16)
        for b in (0, 1):

            def give(b=b):
                low[b] = whole
                for d in low_y[b]:
                    d.start()

            pl.when(is_source[b])(give)

    def low_to_z():
        for b in (0, 1):
            pl.when(at_source & jnp.logical_not(is_source[b]))(lambda b=b: low_y[b][0].wait_recv())

        def give():
            for d in low_z:
                d.start()

        pl.when(at_source)(give)

    local[1].wait()

    half = lax.div(zl, 4)
    half_of = [half, 1 - half, half, 1 - half]
    parity_of = [1 - zh, 1 - zh, zh, zh]
    inside = [lax.div(x, 2) == h for h in half_of]

    def pair_copies(t):
        return [
            rc(psend.at[t, :, :, pl.ds(n, w)], precv.at[t, :, :, pl.ds(n, w)], pss.at[t, s], psr.at[t, s], mate)
            for s, (n, w) in enumerate(GROUPS)
        ]

    def x_copy(t, s, i):
        n, w = GROUPS[s]
        d = 2 * half_of[t] + i
        j = lax.rem(d - x + 3, 4)
        return rc(
            xsend.at[t, i, :, pl.ds(n, w)], xrecv.at[t // 2, j, :, pl.ds(n, w)],
            xss.at[t, s, i], xsr.at[t // 2, s, j], at_row(d, zh, core),
        )

    def leaves(t, i):
        return x != 2 * half_of[t] + i

    def multiply(t):
        for v in range(2):
            k = 4 * half_of[t] + 2 * v + parity_of[t]
            for j in range(3):
                c = k * 4 + lax.rem(y + 3 - j, 4)
                rc(gbuf.at[c], gbuf.at[c], gys.at[k, j], gyr.at[k, j], y_peer[j]).wait_recv()
        for i, c_ in enumerate((1 - core, core)):
            for v in range(2):
                k = 4 * half_of[t] + 2 * v + parity_of[t]
                g = gbuf[pl.ds(k * 4 + 2 * c_, 2)].reshape(32, 1024)
                n = i * 64 + v * 32
                lhs[t, n : n + 32, :] = (g.astype(F32) * scale_v[...]).astype(BF16)
        copies = pair_copies(t)
        for s, (n, w) in enumerate(GROUPS):
            r = jnp.dot(lhs[t], codes_t[:, n : n + w], preferred_element_type=F32)
            psend[t, :, :, n : n + w] = r[0:64].astype(BF16).reshape(2, 32, w)
            copies[s].start()
            acc[t, :, :, n : n + w] = r[64:128].reshape(2, 32, w)

    def to_x(t):
        copies = pair_copies(t)
        for s, (n, w) in enumerate(GROUPS):
            copies[s].wait_recv()
            v = acc[t, :, :, n : n + w] + precv[t, :, :, n : n + w].astype(F32)
            acc[t, :, :, n : n + w] = v
            xsend[t, :, :, n : n + w] = v.astype(BF16)
            for i in range(2):
                pl.when(leaves(t, i))(lambda s=s, i=i: x_copy(t, s, i).start())

    mine = lax.rem(x, 2)

    def x_sum(t, s):
        q = t // 2
        n, w = GROUPS[s]
        for j in range(3):
            rc(
                xrecv.at[q, j, :, pl.ds(n, w)], xrecv.at[q, j, :, pl.ds(n, w)],
                xss.at[t, s, 0], xsr.at[q, s, j], x_peer[j],
            ).wait_recv()
        v = acc[t, pl.ds(mine, 1), :, n : n + w].reshape(32, w)
        for j in range(3):
            v = v + xrecv[q, j, :, n : n + w].astype(F32)
        return v

    z_copies = [
        rc(zsend.at[:, pl.ds(n, w)], zrecv.at[:, pl.ds(n, w)], zss.at[s], zsr.at[s], far)
        for s, (n, w) in enumerate(GROUPS)
    ]

    def to_far(t):
        for s, (n, w) in enumerate(GROUPS):
            zsend[:, n : n + w] = x_sum(t, s).astype(BF16)
            z_copies[s].start()

    def keep(t, s):
        n, w = GROUPS[s]
        total[:, n : n + w] = x_sum(t, s)

    low_to_y()
    multiply(0)
    to_x(0)
    low_to_z()
    multiply(2)
    multiply(1)
    to_x(1)
    multiply(3)
    pl.when(inside[0])(lambda: to_far(0))
    to_x(2)
    to_x(3)

    pl.when(jnp.logical_not(at_source))(lambda: low_z[0].wait_recv())
    rounded = low[...].reshape(32, 128)[:, 0:RANK]
    for c in local[4:]:
        c.wait()
    part = 0.5 * dot_tn(rounded, act_v[...])
    for r in range(16):
        start = r * SLICE
        base, off = start // 128 * 128, start % 128
        if off + SLICE <= 128:
            b = part[:, base : base + 128]
            b = pltpu.roll(b, (128 - off) % 128, 1) if off else b
        else:
            b = pltpu.roll(part[:, base : base + 256], 256 - off, 1)[:, 0:128]
        cblk[r % 2, r // 4, (r // 2) % 2] = b
    c_pair = rc(cblk.at[1 - core], cprecv, cps, cpr, mate)
    c_pair.start()
    pl.when(inside[1])(lambda: to_far(1))
    c_pair.wait_recv()
    cblk[pl.ds(core, 1)] = cblk[pl.ds(core, 1)] + cprecv[...][None]
    c_x = [rc(cblk.at[core, xs[j]], cxrecv.at[j], cxs.at[j], cxr.at[j], x_peer[j]) for j in range(3)]
    for d in c_x:
        d.start()

    def comp_far():
        for d in c_x:
            d.wait_recv()
        v = cblk[pl.ds(core, 1), pl.ds(x, 1)].reshape(2, 16, 128)
        for j in range(3):
            v = v + cxrecv[j]
        czsend[...] = v
        c_far.start()

    c_far = rc(czsend.at[1 - zh], czrecv, czs, czr, far)
    for s, (n, w) in enumerate(GROUPS):
        term = jnp.dot(rounded, down_v[:, n : n + w], preferred_element_type=F32)
        for t in (2, 3):
            pl.when(inside[t])(lambda t=t, s=s: keep(t, s))
        total[:, n : n + w] += 0.5 * term
        if s == 0:
            comp_far()

    for s, (n, w) in enumerate(GROUPS):
        z_copies[s].wait_recv()
        out[:, n : n + w] = (total[:, n : n + w] + zrecv[:, n : n + w].astype(F32)).astype(BF16)
    c_far.wait_recv()
    comp[...] = (czsend[pl.ds(zh, 1)].reshape(16, 128) + czrecv[...])[:, 0:SLICE]

    for d in sends:
        d.wait_send()
    for t in range(4):
        for d in pair_copies(t):
            d.wait_send()
        for i in range(2):

            def sent(t=t, i=i):
                for s in range(NG):
                    x_copy(t, s, i).wait_send()

            pl.when(leaves(t, i))(sent)
    for d in [low_mate, *low_x, low_far, c_pair, c_far, *c_x, *z_copies]:
        d.wait_send()
    for b in (0, 1):
        pl.when(is_source[b])(lambda b=b: [d.wait_send() for d in low_y[b]] and None)
    pl.when(at_source)(lambda: [d.wait_send() for d in low_z] and None)


def write_out(a, b, c, d, sems):
    copies = [pltpu.make_async_copy(a, c, sems.at[0]), pltpu.make_async_copy(b, d, sems.at[1])]
    for v in copies:
        v.start()
    for v in copies:
        v.wait()


def on_device(grad, codes, scale, down, up, act):
    hidden, width = codes.shape
    any_ = pl.BlockSpec(memory_space=pl.ANY)
    vmem = pl.BlockSpec(memory_space=pltpu.VMEM)
    dma = pltpu.SemaphoreType.DMA
    out, comp = pl.pallas_call(
        kernel,
        out_shape=(
            jax.ShapeDtypeStruct((32, hidden), BF16),
            jax.ShapeDtypeStruct((16, SLICE), F32),
        ),
        in_specs=[any_] * 6,
        out_specs=(vmem, vmem),
        scratch_shapes=[
            pltpu.VMEM((32, 16, width), BF16),
            pltpu.VMEM((hidden, width), BF16),
            pltpu.VMEM((width, hidden), BF16),
            pltpu.VMEM((1, width), F32),
            pltpu.VMEM((16, hidden), BF16),
            pltpu.VMEM((16, width), BF16),
            pltpu.VMEM((32, hidden), BF16),
            pltpu.VMEM((4, 128, width), BF16),
            pltpu.VMEM((4, 2, 32, hidden), F32),
            pltpu.VMEM((4, 2, 32, hidden), BF16),
            pltpu.VMEM((4, 2, 32, hidden), BF16),
            pltpu.VMEM((4, 2, 32, hidden), BF16),
            pltpu.VMEM((2, 3, 32, hidden), BF16),
            pltpu.VMEM((32, hidden), BF16),
            pltpu.VMEM((32, hidden), BF16),
            pltpu.VMEM((32, hidden), F32),
            pltpu.VMEM((3, 16, 128), F32),
            pltpu.VMEM((16, 128), F32),
            pltpu.VMEM((3, 16, 128), F32),
            pltpu.VMEM((16, 128), F32),
            pltpu.VMEM((2, 16, 128), BF16),
            pltpu.VMEM((2, 4, 2, 16, 128), F32),
            pltpu.VMEM((4, 2, 16, 128), F32),
            pltpu.VMEM((3, 2, 16, 128), F32),
            pltpu.VMEM((2, 16, 128), F32),
            pltpu.VMEM((16, 128), F32),
            pltpu.SemaphoreType.REGULAR,
            dma((6,)),
            dma((8,)), dma((8,)), dma((8, 3)), dma((8, 3)),
            dma((4, NG)), dma((4, NG)), dma((4, NG, 2)), dma((2, NG, 3)), dma((NG,)), dma((NG,)),
            dma, dma, dma((3,)), dma((3,)), dma, dma, dma((2, 3)), dma((2,)), dma((8,)), dma,
            dma, dma, dma((3,)), dma((3,)), dma, dma,
        ],
        compiler_params=pltpu.CompilerParams(
            collective_id=0, has_side_effects=True, vmem_limit_bytes=60 * 2**20
        ),
        cost_estimate=pl.CostEstimate(flops=2 * 512 * hidden * width, bytes_accessed=4 * 2**20, transcendentals=0),
    )(grad, codes, scale.reshape(1, width), down, up, act)
    return tuple(
        pl.pallas_call(
            write_out,
            out_shape=(
                jax.ShapeDtypeStruct((32, hidden), BF16),
                jax.ShapeDtypeStruct((16, SLICE), F32),
            ),
            in_specs=[vmem, vmem],
            out_specs=(any_, any_),
            scratch_shapes=[dma((2,))],
            compiler_params=pltpu.CompilerParams(has_side_effects=True),
        )(out, comp)
    )


def solution(mesh):
    return jax.shard_map(
        on_device,
        mesh=mesh,
        in_specs=(
            P("col", "row"),
            P("col", "row"),
            P("row"),
            P(None, "col"),
            P(None, "row"),
            P("row", "col"),
        ),
        out_specs=(P("row", "col"), P(None, ("col", "row"))),
        check_vma=False,
    )
```

time: 64.2 us -> 59.3 us (0.924)
  the two profiles are of different devices: /device:TPU:1 before, /device:TPU:24 now
where the time goes in v2:
time: 59.3 us; the launch traced here: 59.2 us
  Pallas kernels  58.5 us (99%)
  between operations  0.64 us (1%)
    pallas_call x1, Pallas kernels, on_device(): pl.pallas_call(kernel, out_shape=(jax.ShapeDtypeStruct((32, hidden), BF16...  57 us
    pallas_call x1, Pallas kernels, on_device(): pl.pallas_call(write_out, out_shape=(jax.ShapeDtypeStruct((32, hidden), B...  1.56 us

profile of v2, /device:TPU:24, one launch (start us, length us, event | category | flops | bytes accessed | tf_op | source)
XLA Modules:
  0.0 59.2 jit_solution(3855550044580611858)
XLA Ops:
  0.6 57.0 %shard_map.77 = (bf16[32,1664]{1,0:T(8,128)(2,1)}, f32[16,104]{1,0:T(8,128)}) custom-call(bf16[16,1024]{1,0:T(8,128)(2,1)} %grad.1, bf16[1664,1024]{1,0:T(8,128)(2,1)} %codes.1, f32[1,1024]{1,0:T(1,128)} %bitcast.1, bf16[16,1664]{1,0:T(8,128)(2,1)} %down.1, bf16[16,1024]{1,0:T(8,128)(2,1)} %up.1, bf16[32,1664]{1,0:T(8,128)(2,1)} %act.1), custom_call_target="tpu_custom_call" | custom-call | flops 1744830464 | bytes 4194304 | tf_op jit(solution)/shard_map/pallas_call | solution.py:333
  57.6 1.6 %shard_map.78 = (bf16[32,1664]{1,0:T(8,128)(2,1)}, f32[16,104]{1,0:T(8,128)}) custom-call(bf16[32,1664]{1,0:T(8,128)(2,1)} %get-tuple-element.4.a, f32[16,104]{1,0:T(8,128)} %get-tuple-element.5.b), custom_call_target="tpu_custom_call" | custom-call | tf_op jit(solution)/shard_map/pallas_call | solution.py:381

commit v3 on v2

--- a/solution.py
+++ b/solution.py
@@ -103,20 +103,33 @@
         c = zmap(m) * 4 + y
         rc(gbuf.at[c], gbuf.at[c], gzs.at[m], gzr.at[m], z_peer[1]).wait_recv()
 
+    odd = 1 - lax.rem(zl + zh, 2)
+
+    def pass_three(base):
+        even_k, odd_k = [zmap(base + 2)], [zmap(base + 1), zmap(base + 3)]
+        for m, k in (
+            (base + 2 - odd, odd * odd_k[0] + (1 - odd) * even_k[0]),
+            (base + 1 + 2 * odd, odd * odd_k[1] + (1 - odd) * odd_k[0]),
+            (base + 3 - odd, odd * even_k[0] + (1 - odd) * odd_k[1]),
+        ):
+            c = k * 4 + y
+            rc(gbuf.at[c], gbuf.at[c], gzs.at[m], gzr.at[m], z_peer[1]).wait_recv()
+            for j in range(3):
+                d = rc(gbuf.at[c], gbuf.at[c], gys.at[k, j], gyr.at[k, j], y_peer[j])
+                d.start()
+                sends.append(d)
+
     pass_on(0, (4, 3, 2, 1))
     low_mate.start()
+    local[1].wait()
     local[3].wait()
     for n in range(0, codes_v.shape[0], 128):
         codes_t[:, n : n + 128] = codes_v[n : n + 128, :].T
-    z_wait(1)
-    pass_on(1, ())
     low_mate.wait_recv()
     lsum[1] = lsum[0] + lmate[...]
     for d in low_x:
         d.start()
-    for m in (2, 3):
-        z_wait(m)
-        pass_on(m, ())
+    pass_three(0)
     lsum[2] = lsum[1]
     for j in range(3):
         low_x[j].wait_recv()
@@ -125,9 +138,6 @@
     low_far.start()
     z_wait(4)
     pass_on(4, (3, 2, 1))
-    for m in (5, 6, 7):
-        z_wait(m)
-        pass_on(m, ())
 
     at_source = zl == 2 * x + zh
     is_source = [at_source & (lax.div(y, 2) == core) & (lax.rem(y, 2) == b) for b in (0, 1)]
@@ -155,8 +165,6 @@
                 d.start()
 
         pl.when(at_source)(give)
-
-    local[1].wait()
 
     half = lax.div(zl, 4)
     half_of = [half, 1 - half, half, 1 - half]
@@ -239,40 +247,34 @@
         n, w = GROUPS[s]
         total[:, n : n + w] = x_sum(t, s)
 
-    low_to_y()
-    multiply(0)
-    to_x(0)
-    low_to_z()
-    multiply(2)
-    multiply(1)
-    to_x(1)
-    multiply(3)
-    pl.when(inside[0])(lambda: to_far(0))
-    to_x(2)
-    to_x(3)
-
-    pl.when(jnp.logical_not(at_source))(lambda: low_z[0].wait_recv())
-    rounded = low[...].reshape(32, 128)[:, 0:RANK]
-    for c in local[4:]:
-        c.wait()
-    part = 0.5 * dot_tn(rounded, act_v[...])
-    for r in range(16):
-        start = r * SLICE
-        base, off = start // 128 * 128, start % 128
-        if off + SLICE <= 128:
-            b = part[:, base : base + 128]
-            b = pltpu.roll(b, (128 - off) % 128, 1) if off else b
-        else:
-            b = pltpu.roll(part[:, base : base + 256], 256 - off, 1)[:, 0:128]
-        cblk[r % 2, r // 4, (r // 2) % 2] = b
     c_pair = rc(cblk.at[1 - core], cprecv, cps, cpr, mate)
-    c_pair.start()
-    pl.when(inside[1])(lambda: to_far(1))
-    c_pair.wait_recv()
-    cblk[pl.ds(core, 1)] = cblk[pl.ds(core, 1)] + cprecv[...][None]
     c_x = [rc(cblk.at[core, xs[j]], cxrecv.at[j], cxs.at[j], cxr.at[j], x_peer[j]) for j in range(3)]
-    for d in c_x:
-        d.start()
+    c_far = rc(czsend.at[1 - zh], czrecv, czs, czr, far)
+
+    def rounded():
+        return low[...].reshape(32, 128)[:, 0:RANK]
+
+    def adapter_gradient():
+        pl.when(jnp.logical_not(at_source))(lambda: low_z[0].wait_recv())
+        for c in local[4:]:
+            c.wait()
+        part = 0.5 * dot_tn(rounded(), act_v[...])
+        for r in range(16):
+            start = r * SLICE
+            base, off = start // 128 * 128, start % 128
+            if off + SLICE <= 128:
+                b = part[:, base : base + 128]
+                b = pltpu.roll(b, (128 - off) % 128, 1) if off else b
+            else:
+                b = pltpu.roll(part[:, base : base + 256], 256 - off, 1)[:, 0:128]
+            cblk[r % 2, r // 4, (r // 2) % 2] = b
+        c_pair.start()
+
+    def comp_x():
+        c_pair.wait_recv()
+        cblk[pl.ds(core, 1)] = cblk[pl.ds(core, 1)] + cprecv[...][None]
+        for d in c_x:
+            d.start()
 
     def comp_far():
         for d in c_x:
@@ -283,14 +285,28 @@
         czsend[...] = v
         c_far.start()
 
-    c_far = rc(czsend.at[1 - zh], czrecv, czs, czr, far)
+    multiply(0)
+    pass_three(4)
+    to_x(0)
+    low_to_y()
+    multiply(2)
+    low_to_z()
+    multiply(1)
+    to_x(1)
+    pl.when(inside[0])(lambda: to_far(0))
+    to_x(2)
+    multiply(3)
+    adapter_gradient()
+    to_x(3)
+    comp_x()
+    pl.when(inside[1])(lambda: to_far(1))
+    comp_far()
+
     for s, (n, w) in enumerate(GROUPS):
-        term = jnp.dot(rounded, down_v[:, n : n + w], preferred_element_type=F32)
+        term = jnp.dot(rounded(), down_v[:, n : n + w], preferred_element_type=F32)
         for t in (2, 3):
             pl.when(inside[t])(lambda t=t, s=s: keep(t, s))
         total[:, n : n + w] += 0.5 * term
-        if s == 0:
-            comp_far()
 
     for s, (n, w) in enumerate(GROUPS):
         z_copies[s].wait_recv()

time: 59.3 us -> 55.8 us (0.941)
  Pallas kernels: 58.5 us -> 54.8 us
    pallas_call x1, Pallas kernels: 57 us -> 53.2 us  [on_device(): pl.pallas_call(kernel, out_shape=(jax.ShapeDtypeStruct((32, hidden), BF16...]
where the time goes in v3:
time: 55.8 us; the launch traced here: 55.4 us
  Pallas kernels  54.8 us (98%)
  between operations  0.64 us (1%)
    pallas_call x1, Pallas kernels, on_device(): pl.pallas_call(kernel, out_shape=(jax.ShapeDtypeStruct((32, hidden), BF16...  53.2 us
    pallas_call x1, Pallas kernels, on_device(): pl.pallas_call(write_out, out_shape=(jax.ShapeDtypeStruct((32, hidden), B...  1.56 us

profile of v3, /device:TPU:24, one launch (start us, length us, event | category | flops | bytes accessed | tf_op | source)
XLA Modules:
  0.0 55.4 jit_solution(5120133575514714782)
XLA Ops:
  0.6 53.2 %shard_map.77 = (bf16[32,1664]{1,0:T(8,128)(2,1)}, f32[16,104]{1,0:T(8,128)}) custom-call(bf16[16,1024]{1,0:T(8,128)(2,1)} %grad.1, bf16[1664,1024]{1,0:T(8,128)(2,1)} %codes.1, f32[1,1024]{1,0:T(1,128)} %bitcast.1, bf16[16,1664]{1,0:T(8,128)(2,1)} %down.1, bf16[16,1024]{1,0:T(8,128)(2,1)} %up.1, bf16[32,1664]{1,0:T(8,128)(2,1)} %act.1), custom_call_target="tpu_custom_call" | custom-call | flops 1744830464 | bytes 4194304 | tf_op jit(solution)/shard_map/pallas_call | solution.py:349
  53.8 1.6 %shard_map.78 = (bf16[32,1664]{1,0:T(8,128)(2,1)}, f32[16,104]{1,0:T(8,128)}) custom-call(bf16[32,1664]{1,0:T(8,128)(2,1)} %get-tuple-element.4.a, f32[16,104]{1,0:T(8,128)} %get-tuple-element.5.b), custom_call_target="tpu_custom_call" | custom-call | tf_op jit(solution)/shard_map/pallas_call | solution.py:397

commit v4 on v3

--- a/solution.py
+++ b/solution.py
@@ -119,7 +119,7 @@
                 d.start()
                 sends.append(d)
 
-    pass_on(0, (4, 3, 2, 1))
+    pass_on(0, (4, 2, 1, 3))
     low_mate.start()
     local[1].wait()
     local[3].wait()

time: 55.8 us -> 55.4 us (level)
  the two profiles are of different devices: /device:TPU:24 before, /device:TPU:2 now
where the time goes in v4:
time: 55.4 us; the launch traced here: 55.2 us
  Pallas kernels  54.6 us (99%)
  between operations  0.64 us (1%)
    pallas_call x1, Pallas kernels, on_device(): pl.pallas_call(kernel, out_shape=(jax.ShapeDtypeStruct((32, hidden), BF16...  53 us
    pallas_call x1, Pallas kernels, on_device(): pl.pallas_call(write_out, out_shape=(jax.ShapeDtypeStruct((32, hidden), B...  1.56 us

profile of v4, /device:TPU:2, one launch (start us, length us, event | category | flops | bytes accessed | tf_op | source)
XLA Modules:
  0.0 55.2 jit_solution(15108134817706190587)
XLA Ops:
  0.6 53.0 %shard_map.77 = (bf16[32,1664]{1,0:T(8,128)(2,1)}, f32[16,104]{1,0:T(8,128)}) custom-call(bf16[16,1024]{1,0:T(8,128)(2,1)} %grad.1, bf16[1664,1024]{1,0:T(8,128)(2,1)} %codes.1, f32[1,1024]{1,0:T(1,128)} %bitcast.1, bf16[16,1664]{1,0:T(8,128)(2,1)} %down.1, bf16[16,1024]{1,0:T(8,128)(2,1)} %up.1, bf16[32,1664]{1,0:T(8,128)(2,1)} %act.1), custom_call_target="tpu_custom_call" | custom-call | flops 1744830464 | bytes 4194304 | tf_op jit(solution)/shard_map/pallas_call | solution.py:349
  53.7 1.6 %shard_map.78 = (bf16[32,1664]{1,0:T(8,128)(2,1)}, f32[16,104]{1,0:T(8,128)}) custom-call(bf16[32,1664]{1,0:T(8,128)(2,1)} %get-tuple-element.4.a, f32[16,104]{1,0:T(8,128)} %get-tuple-element.5.b), custom_call_target="tpu_custom_call" | custom-call | tf_op jit(solution)/shard_map/pallas_call | solution.py:397

commit v5 on v4

--- a/solution.py
+++ b/solution.py
@@ -7,7 +7,7 @@
 
 MESH = pl.DeviceIdType.MESH
 F32, BF16 = jnp.float32, jnp.bfloat16
-GROUPS = ((0, 768), (768, 896))
+GROUPS = ((0, 1024), (1024, 640))
 NG = len(GROUPS)
 SLICE = 104
 RANK = 16

time: 55.4 us -> 55.6 us (level)
  no operation moved by 1% of the time
where the time goes in v5:
time: 55.6 us; the launch traced here: 55.5 us
  Pallas kernels  54.8 us (99%)
  between operations  0.64 us (1%)
    pallas_call x1, Pallas kernels, on_device(): pl.pallas_call(kernel, out_shape=(jax.ShapeDtypeStruct((32, hidden), BF16...  53.3 us
    pallas_call x1, Pallas kernels, on_device(): pl.pallas_call(write_out, out_shape=(jax.ShapeDtypeStruct((32, hidden), B...  1.56 us

profile of v5, /device:TPU:2, one launch (start us, length us, event | category | flops | bytes accessed | tf_op | source)
XLA Modules:
  0.0 55.5 jit_solution(120015808742575486)
XLA Ops:
  0.6 53.3 %shard_map.77 = (bf16[32,1664]{1,0:T(8,128)(2,1)}, f32[16,104]{1,0:T(8,128)}) custom-call(bf16[16,1024]{1,0:T(8,128)(2,1)} %grad.1, bf16[1664,1024]{1,0:T(8,128)(2,1)} %codes.1, f32[1,1024]{1,0:T(1,128)} %bitcast.1, bf16[16,1664]{1,0:T(8,128)(2,1)} %down.1, bf16[16,1024]{1,0:T(8,128)(2,1)} %up.1, bf16[32,1664]{1,0:T(8,128)(2,1)} %act.1), custom_call_target="tpu_custom_call" | custom-call | flops 1744830464 | bytes 4194304 | tf_op jit(solution)/shard_map/pallas_call | solution.py:349
  53.9 1.6 %shard_map.78 = (bf16[32,1664]{1,0:T(8,128)(2,1)}, f32[16,104]{1,0:T(8,128)}) custom-call(bf16[32,1664]{1,0:T(8,128)(2,1)} %get-tuple-element.4.a, f32[16,104]{1,0:T(8,128)} %get-tuple-element.5.b), custom_call_target="tpu_custom_call" | custom-call | tf_op jit(solution)/shard_map/pallas_call | solution.py:397
